TPU v7x, 32 devices: a whole 2x2x4 slice. The times are simulated.
32 devices in a mesh: seq: 8 (over z, y), blk: 4 (over x, core).
Axes of the slice: x: 2, y: 2, z: 4, core: 2. Of those that a mesh axis runs over, the one named last changes fastest.
Arguments:
- hidden_in: bfloat16 [16, 1024, 768], P('seq', 'blk'), may hold values from -6 to 6
- depth_group: int32 [16], P('seq'), may hold values from 0 to 2
- query_weight: bfloat16 [768, 768], replicated, may hold values from -0.21875 to 0.21875
- query_bias: bfloat16 [768], replicated, may hold values from -3 to 3
- key_weight: bfloat16 [768, 768], replicated, may hold values from -0.21875 to 0.21875
- value_weight: bfloat16 [768, 768], replicated, may hold values from -0.21875 to 0.21875
- value_bias: bfloat16 [768], replicated, may hold values from -0.119628906 to 0.119628906
- output_weight: bfloat16 [768, 768], replicated, may hold values from -4 to 4
- output_bias: bfloat16 [768], replicated, may hold values from -3 to 3
- attn_gain: bfloat16 [768], replicated, may hold values from 0.5 to 1.5
- attn_shift: bfloat16 [768], replicated, may hold values from -3 to 3
- inner_weight: bfloat16 [768, 3072], replicated, may hold values from -0.21875 to 0.21875
- inner_bias: bfloat16 [3072], replicated, may hold values from -3 to 3
- outer_weight: bfloat16 [3072, 768], replicated, may hold values from -0.109375 to 0.109375
- outer_bias: bfloat16 [768], replicated, may hold values from -3 to 3
- final_gain: bfloat16 [768], replicated, may hold values from 0.5 to 1.5
- final_shift: bfloat16 [768], replicated, may hold values from -3 to 3
- grad_out: bfloat16 [16, 1024, 768], P('seq', 'blk'), may hold values from -6 to 6
Outputs:
- hidden_out: bfloat16 [16, 1024, 768], P('seq', 'blk')
- grad_in: bfloat16 [16, 1024, 768], P('seq', 'blk')
- grad_query_weight: float32 [768, 768], P('seq')
- grad_query_bias: float32 [768], P('seq')
- grad_key_weight: float32 [768, 768], P('seq')
- grad_value_weight: float32 [768, 768], P('seq')
- grad_value_bias: float32 [768], P('seq')
- grad_output_weight: float32 [768, 768], P('seq')
- grad_output_bias: float32 [768], P('seq')
- grad_attn_gain: float32 [768], P('seq')
- grad_attn_shift: float32 [768], P('seq')
- grad_inner_weight: float32 [768, 3072], P('seq')
- grad_inner_bias: float32 [3072], P('seq')
- grad_outer_weight: float32 [3072, 768], P('seq')
- grad_outer_bias: float32 [768], P('seq')
- grad_final_gain: float32 [768], P('seq')
- grad_final_shift: float32 [768], P('seq')
All inputs are finite; a program needn't handle non-finite values.
Results may differ from a plain program's by a relative error of at most 0.02.
Values may be sent and summed in bfloat16 or wider, within the bound.
A program may use at most 128 MiB of HBM per device.

v0:
```python
import jax
import jax.numpy as jnp
from jax import lax
from jax.sharding import PartitionSpec as P

HEADS = 12
HD = 64


def layer_norm(values, gain, shift):
    row_mean = jnp.mean(values, axis=-1, keepdims=True)
    centered = values - row_mean
    variance = jnp.mean(centered * centered, axis=-1, keepdims=True)
    return centered * lax.rsqrt(variance + 1e-05) * gain + shift


def gelu_exact(values):
    return jax.nn.gelu(values, approximate=False)


def row_dot(left, right):
    return jnp.dot(left, right, preferred_element_type=jnp.float32)


def left_dot(left, right):
    return lax.dot_general(
        left, right, (((0,), (0,)), ((), ())), preferred_element_type=jnp.float32
    )


def right_dot(left, right):
    return lax.dot_general(
        left, right, (((1,), (1,)), ((), ())), preferred_element_type=jnp.float32
    )


def column_sums(matrix):
    return jnp.sum(matrix.astype(jnp.float32), axis=0)


def attention_back(members):
    query_seq, key_seq, value_seq, lse_seq, upstream = members
    scores = 0.125 * jnp.einsum(
        "qhd,khd->hqk", query_seq, key_seq, preferred_element_type=jnp.float32
    )
    probs = jnp.exp(scores - lse_seq[..., None])
    grad_probs = jnp.einsum("qhd,khd->hqk", upstream, value_seq, preferred_element_type=jnp.float32)
    center = jnp.sum(probs * grad_probs, axis=-1, keepdims=True)
    grad_scores = (probs * (grad_probs - center)).astype(jnp.bfloat16)
    grad_query = 0.125 * jnp.einsum(
        "hqk,khd->qhd", grad_scores, key_seq, preferred_element_type=jnp.float32
    )
    grad_key = 0.125 * jnp.einsum(
        "hqk,qhd->khd", grad_scores, query_seq, preferred_element_type=jnp.float32
    )
    grad_value = jnp.einsum(
        "hqk,qhd->khd", probs.astype(jnp.bfloat16), upstream, preferred_element_type=jnp.float32
    )
    return (grad_query, grad_key, grad_value)


def local(
    hidden_in,
    depth_group,
    query_weight,
    query_bias,
    key_weight,
    value_weight,
    value_bias,
    output_weight,
    output_bias,
    attn_gain,
    attn_shift,
    inner_weight,
    inner_bias,
    outer_weight,
    outer_bias,
    final_gain,
    final_shift,
    grad_out,
):
    seq_dev, local_tok, width = hidden_in.shape
    row_count = seq_dev * local_tok
    kept_rows = jnp.repeat((depth_group != 2).astype(jnp.float32), local_tok)[:, None]
    x_rows = hidden_in.reshape(row_count, width)
    x_float = x_rows.astype(jnp.float32)
    queries = (row_dot(x_rows, query_weight) + query_bias.astype(jnp.float32)).astype(jnp.bfloat16)
    keys_local = row_dot(x_rows, key_weight).astype(jnp.bfloat16).reshape(seq_dev, local_tok, width)
    values_local = (row_dot(x_rows, value_weight) + value_bias.astype(jnp.float32)).astype(
        jnp.bfloat16
    )
    values_local = values_local.reshape(seq_dev, local_tok, width)
    query_heads = queries.reshape(seq_dev, local_tok, HEADS, HD)
    arrived = (
        lax.all_gather(keys_local, "blk", axis=1, tiled=True),
        lax.all_gather(values_local, "blk", axis=1, tiled=True),
    )
    run_max = jnp.full((seq_dev, HEADS, local_tok), -1e30, jnp.float32)
    key_total = arrived[0].shape[1]
    key_heads = arrived[0].reshape(seq_dev, key_total, HEADS, HD)
    value_heads = arrived[1].reshape(seq_dev, key_total, HEADS, HD)
    scores = 0.125 * jnp.einsum(
        "bqhd,bkhd->bhqk", query_heads, key_heads, preferred_element_type=jnp.float32
    )
    new_max = jnp.maximum(run_max, jnp.max(scores, axis=-1))
    weights = jnp.exp(scores - new_max[..., None])
    new_sum = jnp.sum(weights, axis=-1)
    accum = jnp.einsum(
        "bhqk,bkhd->bqhd",
        weights.astype(jnp.bfloat16),
        value_heads,
        preferred_element_type=jnp.float32,
    )
    run_max, run_sum, accum = (new_max, new_sum, accum)
    attended = accum / jnp.transpose(run_sum, (0, 2, 1))[..., None]
    attended_low = attended.reshape(row_count, width).astype(jnp.bfloat16)
    log_sum = run_max + jnp.log(run_sum)
    attn_out = row_dot(attended_low, output_weight) + output_bias.astype(jnp.float32)
    normed, first_pull = jax.vjp(
        layer_norm,
        x_float + attn_out,
        attn_gain.astype(jnp.float32),
        attn_shift.astype(jnp.float32),
    )
    inner_in = normed.astype(jnp.bfloat16)
    pre_act = row_dot(inner_in, inner_weight) + inner_bias.astype(jnp.float32)
    activated, gelu_pull = jax.vjp(gelu_exact, pre_act)
    act_low = activated.astype(jnp.bfloat16)
    ffn_out = row_dot(act_low, outer_weight) + outer_bias.astype(jnp.float32)
    result, second_pull = jax.vjp(
        layer_norm,
        normed + ffn_out,
        final_gain.astype(jnp.float32),
        final_shift.astype(jnp.float32),
    )
    hidden_out = (kept_rows * result + (1.0 - kept_rows) * x_float).astype(jnp.bfloat16)
    grad_rows = grad_out.reshape(row_count, width).astype(jnp.float32)
    grad_sum2, grad_final_gain, grad_final_shift = second_pull(kept_rows * grad_rows)
    grad_ffn = grad_sum2.astype(jnp.bfloat16)
    grad_outer_bias = column_sums(grad_ffn)
    grad_outer_weight = left_dot(act_low, grad_ffn)
    (grad_pre,) = gelu_pull(right_dot(grad_ffn, outer_weight))
    grad_pre_low = grad_pre.astype(jnp.bfloat16)
    grad_inner_bias = column_sums(grad_pre_low)
    grad_inner_weight = left_dot(inner_in, grad_pre_low)
    grad_normed = grad_sum2 + right_dot(grad_pre_low, inner_weight)
    grad_sum1, grad_attn_gain, grad_attn_shift = first_pull(grad_normed)
    grad_attn = grad_sum1.astype(jnp.bfloat16)
    grad_output_bias = column_sums(grad_attn)
    grad_output_weight = left_dot(attended_low, grad_attn)
    grad_attended = right_dot(grad_attn, output_weight).astype(jnp.bfloat16)
    keys_whole, values_whole = (
        lax.all_gather(keys_local, "blk", axis=1, tiled=True),
        lax.all_gather(values_local, "blk", axis=1, tiled=True),
    )
    seq_tokens = keys_whole.shape[1]
    key_heads_all = keys_whole.reshape(seq_dev, seq_tokens, HEADS, HD)
    value_heads_all = values_whole.reshape(seq_dev, seq_tokens, HEADS, HD)
    upstream_heads = grad_attended.reshape(seq_dev, local_tok, HEADS, HD)
    grad_query, grad_key_part, grad_value_part = lax.map(
        attention_back, (query_heads, key_heads_all, value_heads_all, log_sum, upstream_heads)
    )
    grad_key_home, grad_value_home = (
        lax.psum_scatter(
            grad_key_part.reshape(seq_dev, seq_tokens, width).astype(jnp.bfloat16),
            "blk",
            scatter_dimension=1,
            tiled=True,
        ).astype(jnp.float32),
        lax.psum_scatter(
            grad_value_part.reshape(seq_dev, seq_tokens, width).astype(jnp.bfloat16),
            "blk",
            scatter_dimension=1,
            tiled=True,
        ).astype(jnp.float32),
    )
    grad_key_low = grad_key_home.reshape(row_count, width).astype(jnp.bfloat16)
    grad_value_low = grad_value_home.reshape(row_count, width).astype(jnp.bfloat16)
    grad_query_low = grad_query.reshape(row_count, width).astype(jnp.bfloat16)
    grad_query_weight = left_dot(x_rows, grad_query_low)
    grad_query_bias = column_sums(grad_query_low)
    grad_key_weight = left_dot(x_rows, grad_key_low)
    grad_value_weight = left_dot(x_rows, grad_value_low)
    grad_value_bias = column_sums(grad_value_low)
    grad_input = (
        grad_sum1
        + right_dot(grad_query_low, query_weight)
        + right_dot(grad_key_low, key_weight)
        + right_dot(grad_value_low, value_weight)
        + (1.0 - kept_rows) * grad_rows
    )
    grad_in = grad_input.astype(jnp.bfloat16).reshape(seq_dev, local_tok, width)
    shares = (
        lax.psum_scatter(grad_query_weight, "seq", scatter_dimension=0, tiled=True),
        lax.psum_scatter(grad_query_bias, "seq", scatter_dimension=0, tiled=True),
        lax.psum_scatter(grad_key_weight, "seq", scatter_dimension=0, tiled=True),
        lax.psum_scatter(grad_value_weight, "seq", scatter_dimension=0, tiled=True),
        lax.psum_scatter(grad_value_bias, "seq", scatter_dimension=0, tiled=True),
        lax.psum_scatter(grad_output_weight, "seq", scatter_dimension=0, tiled=True),
        lax.psum_scatter(grad_output_bias, "seq", scatter_dimension=0, tiled=True),
        lax.psum_scatter(grad_attn_gain, "seq", scatter_dimension=0, tiled=True),
        lax.psum_scatter(grad_attn_shift, "seq", scatter_dimension=0, tiled=True),
        lax.psum_scatter(grad_inner_weight, "seq", scatter_dimension=0, tiled=True),
        lax.psum_scatter(grad_inner_bias, "seq", scatter_dimension=0, tiled=True),
        lax.psum_scatter(grad_outer_weight, "seq", scatter_dimension=0, tiled=True),
        lax.psum_scatter(grad_outer_bias, "seq", scatter_dimension=0, tiled=True),
        lax.psum_scatter(grad_final_gain, "seq", scatter_dimension=0, tiled=True),
        lax.psum_scatter(grad_final_shift, "seq", scatter_dimension=0, tiled=True),
    )
    summed = (
        lax.psum(shares[0].astype(jnp.bfloat16), "blk").astype(jnp.float32),
        lax.psum(shares[1].astype(jnp.bfloat16), "blk").astype(jnp.float32),
        lax.psum(shares[2].astype(jnp.bfloat16), "blk").astype(jnp.float32),
        lax.psum(shares[3].astype(jnp.bfloat16), "blk").astype(jnp.float32),
        lax.psum(shares[4].astype(jnp.bfloat16), "blk").astype(jnp.float32),
        lax.psum(shares[5].astype(jnp.bfloat16), "blk").astype(jnp.float32),
        lax.psum(shares[6].astype(jnp.bfloat16), "blk").astype(jnp.float32),
        lax.psum(shares[7].astype(jnp.bfloat16), "blk").astype(jnp.float32),
        lax.psum(shares[8].astype(jnp.bfloat16), "blk").astype(jnp.float32),
        lax.psum(shares[9].astype(jnp.bfloat16), "blk").astype(jnp.float32),
        lax.psum(shares[10].astype(jnp.bfloat16), "blk").astype(jnp.float32),
        lax.psum(shares[11].astype(jnp.bfloat16), "blk").astype(jnp.float32),
        lax.psum(shares[12].astype(jnp.bfloat16), "blk").astype(jnp.float32),
        lax.psum(shares[13].astype(jnp.bfloat16), "blk").astype(jnp.float32),
        lax.psum(shares[14].astype(jnp.bfloat16), "blk").astype(jnp.float32),
    )
    return (
        hidden_out.reshape(seq_dev, local_tok, width),
        grad_in,
        summed[0],
        summed[1],
        summed[2],
        summed[3],
        summed[4],
        summed[5],
        summed[6],
        summed[7],
        summed[8],
        summed[9],
        summed[10],
        summed[11],
        summed[12],
        summed[13],
        summed[14],
    )


def solution(mesh):
    placed = (
        P("seq", "blk", None),
        P("seq"),
        P(),
        P(),
        P(),
        P(),
        P(),
        P(),
        P(),
        P(),
        P(),
        P(),
        P(),
        P(),
        P(),
        P(),
        P(),
        P("seq", "blk", None),
    )
    return jax.shard_map(
        local,
        mesh=mesh,
        in_specs=placed,
        out_specs=(
            P("seq", "blk", None),
            P("seq", "blk", None),
            P("seq", None),
            P("seq"),
            P("seq", None),
            P("seq", None),
            P("seq"),
            P("seq", None),
            P("seq"),
            P("seq"),
            P("seq"),
            P("seq", None),
            P("seq"),
            P("seq", None),
            P("seq"),
            P("seq"),
            P("seq"),
        ),
        check_vma=False,
    )
```

profile of v0, /device:TPU:1, one launch (start us, length us, event | category | flops | bytes accessed | tf_op | source)
XLA Modules:
  0.0 957.5 jit_solution(5737413435974727283)
XLA Ops:
  7.3 3.3 convolution_convert_fusion.1
  10.7 2.9 add_convert_fusion.2
  13.8 2.1 add_convert_fusion.1
  23.5 18.3 %all-gather.5.cloned.1.call-done = bf16[2,1024,768]{2,1,0:T(8,128)(2,1)} async-done(((bf16[2,256,768]{2,1,0:T(8,128)(2,1)}), bf16[2,1024,768]{2,1,0:T(8,128)(2,1)}) %all-gather.5.cloned.1.call-update) | async-done | bytes 3145744 | tf_op jit(solution)/shard_map/all_gather | solution.py:95
  41.8 5.2 copy.75
  46.9 12.5 %multiply_reduce_fusion.1 = (f32[2,12,256]{2,1,0:T(8,128)S(1)}, f32[2,12,256,1024]{3,2,1,0:T(8,128)}) fusion(bf16[2,1024,12,64]{1,3,2,0:T(8,128)(2,1)} %bitcast.178, bf16[2,256,12,64]{1,0,3,2:T(2,128)(2,1)S(1)} %reshape.174), kind=kOutput, calls=%fused_computation.37 | convolution fusion | flops 817883136 | bytes 29122560 | tf_op jit(solution)/shard_map/bqhd,bkhd->bhqk/dot_general | solution.py:102
  59.4 11.0 %fusion.39 = f32[2,12,256]{2,1,0:T(8,128)S(1)} fusion(f32[2,12,256,1024]{3,2,1,0:T(8,128)} %get-tuple-element.236, f32[2,12,256]{2,1,0:T(8,128)S(1)} %broadcast_maximum_fusion), kind=kLoop, calls=%fused_computation.38 | loop fusion | flops 18868224 | bytes 25214976 | tf_op jit(solution)/shard_map/reduce_sum | solution.py:107
  72.5 4.7 copy.73
  77.1 11.6 %fusion.62 = bf16[2,256,12,64]{1,3,2,0:T(8,128)(2,1)S(1)} fusion(bf16[2,1024,12,64]{1,3,2,0:T(8,128)(2,1)} %bitcast.180, f32[2,12,256,1024]{3,2,1,0:T(8,128)} %get-tuple-element.236, f32[2,12,256]{2,1,0:T(8,128)S(1)} %broadcast_maximum_fusion, f32[2,256,12]{1,2,0:T(8,128)S(1)} %bitcast.200), kind=kOutput, calls=%fused_computation.83 | convolution fusion | flops 824967168 | bytes 29147136 | tf_op jit(solution)/shard_map/bhqk,bkhd->bqhd/dot_general | solution.py:108
  91.2 20.4 %multiply_convert_fusion.1 = (bf16[512,3072]{1,0:T(8,128)(2,1)S(1)}, f32[512,3072]{1,0:T(8,128)}, f32[512,3072]{1,0:T(8,128)}) fusion(f32[3072]{0:T(1024)S(1)} %copy-done.45, bf16[768,3072]{1,0:T(8,128)(2,1)} %param.31, f32[512,768]{1,0:T(8,128)S(1)} %get-tuple-element.238, f32[768]{0:T(1024)S(1)} %copy-done.50, f32[768]{0:T(1024)S(1)} %convert_element_type.241, ...), kind=kOutput, calls=%fused_computation.47 | convolution fusion | flops 2521694208 | bytes 22042624 | tf_op jit(solution)/shard_map/dot_general | solution.py:22
  111.6 2.8 fusion.79
  118.7 9.8 %convert_reduce_fusion = (f32[3072]{0:T(1024)}, bf16[512,3072]{1,0:T(8,128)(2,1)}) fusion(f32[512,3072]{1,0:T(8,128)} %get-tuple-element.231, f32[512,3072]{1,0:T(8,128)} %get-tuple-element.239, f32[3072]{0:T(1024)S(1)} %copy-done.45, bf16[512,768]{1,0:T(8,128)(2,1)S(1)} %get-tuple-element.221, bf16[3072,768]{1,0:T(8,128)(2,1)S(1)} %bitcast.205), kind=kOutput, calls=%fused_computation.45 | convolution fusion | flops 2442654720 | bytes 21258240 | tf_op jit(solution)/shard_map/dot_general | solution.py:32
  128.6 5.7 multiply_reduce_fusion.2
  139.8 47.7 %while.14 = (s32[]{:T(128)}, bf16[2,256,12,64]{1,3,2,0:T(8,128)(2,1)S(1)}, bf16[2,1024,12,64]{1,3,2,0:T(8,128)(2,1)}, bf16[2,1024,12,64]{1,3,2,0:T(8,128)(2,1)},...) while((s32[]{:T(128)}, ...), condition=%wide.region_12.0_spmd, body=%wide.region_10.12_spmd.sunk | while | flops 2051994624 | bytes 158172384 | solution.py:160
  140.0 3.4 fusion.140
  143.4 6.3 multiply_reduce_fusion.7
  149.7 6.6 multiply_convert_fusion.3
  158.2 2.0 fusion.141
  160.3 3.5 bitcast_dynamic-update-slice_fusion.5
  163.7 3.4 fusion.140
  167.1 6.3 multiply_reduce_fusion.7
  173.4 6.6 multiply_convert_fusion.3
  181.9 2.0 fusion.141
  184.0 3.5 bitcast_dynamic-update-slice_fusion.5
  189.1 2.3 fusion.82
  194.1 2.0 copy.87
  196.2 29.0 %reduce-scatter.15.cloned.1.call-done = bf16[2,256,768]{1,2,0:T(8,128)(2,1)} async-done(((bf16[2,1024,768]{1,2,0:T(8,128)(2,1)}), bf16[2,256,768]{1,2,0:T(8,128)(2,1)}) %reduce-scatter.15.cloned.1.call-update) | async-done | bytes 786448 | tf_op jit(solution)/shard_map/reduce_scatter | solution.py:164
  227.1 2.0 copy.89
  229.4 36.3 %reduce-scatter.17.cloned.1.call-done = bf16[2,256,768]{1,2,0:T(8,128)(2,1)} async-done(((bf16[2,1024,768]{1,2,0:T(8,128)(2,1)}), bf16[2,256,768]{1,2,0:T(8,128)(2,1)}) %reduce-scatter.17.cloned.1.call-update) | async-done | bytes 786448 | tf_op jit(solution)/shard_map/reduce_scatter | solution.py:170
  267.7 1.9 copy.91
  269.7 8.2 fusion.83
  279.3 7.2 fusion.71
  289.7 3.3 fusion.80
  293.0 44.1 %reduce-scatter.19.cloned.1.call-done = f32[96,768]{1,0:T(8,128)} async-done(((f32[768,768]{1,0:T(8,128)}), f32[96,768]{1,0:T(8,128)}) %reduce-scatter.19.cloned.1.call-update) | async-done | bytes 294928 | tf_op jit(solution)/shard_map/reduce_scatter | solution.py:199
  338.7 70.0 %reduce-scatter.25.cloned.1.call-done = f32[96,768]{1,0:T(8,128)} async-done(((f32[768,768]{1,0:T(8,128)}), f32[96,768]{1,0:T(8,128)}) %reduce-scatter.25.cloned.1.call-update) | async-done | bytes 294928
  410.4 70.0 %reduce-scatter.27.cloned.1.call-done = f32[96,768]{1,0:T(8,128)} async-done(((f32[768,768]{1,0:T(8,128)}), f32[96,768]{1,0:T(8,128)}) %reduce-scatter.27.cloned.1.call-update) | async-done | bytes 294928
  482.2 70.0 %reduce-scatter.29.cloned.1.call-done = f32[96,768]{1,0:T(8,128)} async-done(((f32[768,768]{1,0:T(8,128)}), f32[96,768]{1,0:T(8,128)}) %reduce-scatter.29.cloned.1.call-update) | async-done | bytes 294928
  554.0 165.3 %reduce-scatter.23.cloned.1.call-done = f32[384,768]{1,0:T(8,128)} async-done(((f32[3072,768]{1,0:T(8,128)}), f32[384,768]{1,0:T(8,128)}) %reduce-scatter.23.cloned.1.call-update) | async-done | bytes 1179664 | tf_op jit(solution)/shard_map/reduce_scatter | solution.py:205
  719.3 2.2 convert_element_type.291
  721.5 163.9 %reduce-scatter.21.cloned.1.call-done = f32[96,3072]{1,0:T(8,128)} async-done(((f32[768,3072]{1,0:T(8,128)}), f32[96,3072]{1,0:T(8,128)}) %reduce-scatter.21.cloned.1.call-update) | async-done | bytes 1179664 | tf_op jit(solution)/shard_map/reduce_scatter | solution.py:203
  885.4 2.2 convert_element_type.286
  887.8 28.6 %all-reduce.9 = (bf16[768]{0:T(1024)(128)(2,1)S(1)}, bf16[768]{0:T(1024)(128)(2,1)S(1)}, bf16[768]{0:T(1024)(128)(2,1)S(1)}, bf16[768]{0:T(1024)(128)(2,1)S(1)},...) all-reduce(f32[768]{0:T(1024)S(1)} %reduce_sum.189, ...), channel_id=5, replica_groups=mesh['seq'=8,'blk'=4] {'seq'}, use_global_device_ids=true, to_apply=%region_18.0.clone | all-reduce | flops 9216 | bytes 55296
  917.1 12.9 %all-reduce.10 = (bf16[96]{0:T(256)(128)(2,1)S(1)}, bf16[96]{0:T(256)(128)(2,1)S(1)}, bf16[96]{0:T(256)(128)(2,1)S(1)}, bf16[96]{0:T(256)(128)(2,1)S(1)}, bf16[9...) all-reduce(bf16[96]{0:T(256)(128)(2,1)S(1)} %dynamic-slice.35, ...), channel_id=1, replica_groups=mesh['seq'=8,'blk'=4] {'blk'}, use_global_device_ids=true, to_apply=%region_19.0 | all-reduce | flops 1152 | bytes 4608 | tf_op jit(solution)/shard_map/psum | solution.py:212
  934.7 2.4 copy.82
  938.2 2.5 fusion.81
  940.8 1.9 fusion.61
  942.8 2.2 convert_element_type.287
  945.0 2.2 convert_element_type.292
  (251 shorter events, 54.5 us)
Async XLA Ops:
  7.2 82.6 %copy-start = (bf16[768,768]{1,0:T(8,128)(2,1)S(1)}, bf16[768,768]{1,0:T(8,128)(2,1)}, u32[]{:S(2)}) copy-start(bf16[768,768]{1,0:T(8,128)(2,1)} %param.27) | copy-start | bytes 3538948
  7.2 3.5 copy-start.8
  7.2 3.4 copy-start.56
  7.2 34.5 %all-gather.5.cloned.1.call-start = ((), (), s32[]{:S(2)}) async-start(), calls=%async_computation.9 | async-start | bytes 3932160 | tf_op jit(solution)/shard_map/all_gather | solution.py:95
  10.6 3.1 copy-start.57
  10.6 61.9 %all-gather.3.cloned.1.call-start = ((), (), s32[]{:S(2)}) async-start(), calls=%async_computation.8 | async-start | bytes 3932160 | tf_op jit(solution)/shard_map/all_gather | solution.py:96
  13.6 211.5 %reduce-scatter.15.cloned.1.call-start = ((), (), s32[]{:S(2)}) async-start(), calls=%async_computation.10 | async-start | bytes 3932160 | tf_op jit(solution)/shard_map/reduce_scatter | solution.py:164
  13.7 5.1 copy-start.49
  17.6 116.7 %copy-start.43 = (f32[768]{0:T(1024)}, f32[768]{0:T(1024)S(1)}, u32[]{:S(2)}) copy-start(f32[768]{0:T(1024)S(1)} %convert_element_type.241) | copy-start | bytes 9220
  89.8 21.7 %slice-start = ((s8[4718592]{0:T(1024)(128)(4,1)}), s8[4194304]{0:T(1024)(128)(4,1)S(1)}, s32[]{:S(2)}) async-start(s8[4718592]{0:T(1024)(128)(4,1)} %bitcast.204), calls=%async_computation.19 | async-start | bytes 8388608
  90.8 43.5 %copy-start.11 = (f32[512,768]{1,0:T(8,128)}, f32[512,768]{1,0:T(8,128)S(1)}, u32[]{:S(2)}) copy-start(f32[512,768]{1,0:T(8,128)S(1)} %get-tuple-element.238) | copy-start | bytes 4718596
  90.8 43.5 %copy-start.36 = (f32[512]{0:T(512)}, f32[512]{0:T(512)S(1)}, u32[]{:S(2)}) copy-start(f32[512]{0:T(512)S(1)} %broadcast_multiply_fusion.1) | copy-start | bytes 6148
  91.2 43.2 %copy-start.47 = (f32[512]{0:T(512)}, f32[512]{0:T(512)S(1)}, u32[]{:S(2)}) copy-start(f32[512]{0:T(512)S(1)} %fusion.66) | copy-start | bytes 6148
  91.2 20.4 %copy-start.52 = (f32[768]{0:T(1024)S(1)}, f32[768]{0:T(1024)}, u32[]{:S(2)}) copy-start(f32[768]{0:T(1024)} %convert_element_type.246) | copy-start | bytes 9220
  91.2 20.4 %slice-start.1 = ((s8[4718592]{0:T(1024)(128)(4,1)}), s8[524288]{0:T(1024)(128)(4,1)S(1)}, s32[]{:S(2)}) async-start(s8[4718592]{0:T(1024)(128)(4,1)} %bitcast.204), calls=%async_computation.20 | async-start | bytes 1048576
  111.6 3.2 copy-start.6
  116.0 12.5 %slice-start.2 = ((s8[4718592]{0:T(1024)(128)(4,1)}), s8[4194304]{0:T(1024)(128)(4,1)S(1)}, s32[]{:S(2)}) async-start(s8[4718592]{0:T(1024)(128)(4,1)} %bitcast.206), calls=%async_computation.21 | async-start | bytes 8388608
  118.7 9.8 %copy-start.27 = (bf16[512,768]{1,0:T(8,128)(2,1)}, bf16[512,768]{1,0:T(8,128)(2,1)S(1)}, u32[]{:S(2)}) copy-start(bf16[512,768]{1,0:T(8,128)(2,1)S(1)} %get-tuple-element.221) | copy-start | bytes 2359300
  118.7 9.8 %slice-start.3 = ((s8[4718592]{0:T(1024)(128)(4,1)}), s8[524288]{0:T(1024)(128)(4,1)S(1)}, s32[]{:S(2)}) async-start(s8[4718592]{0:T(1024)(128)(4,1)} %bitcast.206), calls=%async_computation.22 | async-start | bytes 1048576
  140.0 3.4 copy-start.3
  149.7 6.7 copy-start.14
  163.7 3.4 copy-start.3
  173.4 6.7 copy-start.14
  187.5 4.0 copy-start.17
  187.5 78.3 %reduce-scatter.17.cloned.1.call-start = ((), (), s32[]{:S(2)}) async-start(), calls=%async_computation.11 | async-start | bytes 3932160 | tf_op jit(solution)/shard_map/reduce_scatter | solution.py:170
  188.1 149.0 %reduce-scatter.19.cloned.1.call-start = ((), (), s32[]{:S(2)}) async-start(), calls=%async_computation.12 | async-start | bytes 2654208 | tf_op jit(solution)/shard_map/reduce_scatter | solution.py:199
  191.4 217.3 %reduce-scatter.25.cloned.1.call-start = ((), (), s32[]{:S(2)}) async-start(), calls=%async_computation.15 | async-start | bytes 2654208
  196.1 284.3 %reduce-scatter.27.cloned.1.call-start = ((), (), s32[]{:S(2)}) async-start(), calls=%async_computation.16 | async-start | bytes 2654208
  229.1 323.1 %reduce-scatter.29.cloned.1.call-start = ((), (), s32[]{:S(2)}) async-start(), calls=%async_computation.17 | async-start | bytes 2654208
  269.6 449.7 %reduce-scatter.23.cloned.1.call-start = ((), (), s32[]{:S(2)}) async-start(), calls=%async_computation.14 | async-start | bytes 10616832 | tf_op jit(solution)/shard_map/reduce_scatter | solution.py:205
  277.9 607.4 %reduce-scatter.21.cloned.1.call-start = ((), (), s32[]{:S(2)}) async-start(), calls=%async_computation.13 | async-start | bytes 10616832 | tf_op jit(solution)/shard_map/reduce_scatter | solution.py:203
  286.5 3.2 copy-start.22
  286.5 656.2 %all-reduce.14.cloned.1.call-start = ((), (), s32[]{:S(2)}) async-start(), calls=%async_computation.18 | async-start | bytes 3833856 | tf_op jit(solution)/shard_map/psum | solution.py:211
  410.4 477.1 %copy-start.10 = (bf16[2,256,768]{1,2,0:T(8,128)(2,1)S(1)}, bf16[2,256,768]{1,2,0:T(8,128)(2,1)}, u32[]{:S(2)}) copy-start(bf16[2,256,768]{1,2,0:T(8,128)(2,1)} %reduce-scatter.17.cloned.1.call-done) | copy-start | bytes 2359300
  554.0 333.8 %copy-start.40 = (f32[768]{0:T(1024)S(1)}, f32[768]{0:T(1024)}, u32[]{:S(2)}) copy-start(f32[768]{0:T(1024)} %get-tuple-element.175) | copy-start | bytes 9220
  554.0 333.8 %copy-start.41 = (f32[768]{0:T(1024)S(1)}, f32[768]{0:T(1024)}, u32[]{:S(2)}) copy-start(f32[768]{0:T(1024)} %get-tuple-element.220) | copy-start | bytes 9220
  554.0 333.8 %copy-start.42 = (f32[768]{0:T(1024)S(1)}, f32[768]{0:T(1024)}, u32[]{:S(2)}) copy-start(f32[768]{0:T(1024)} %get-tuple-element.224) | copy-start | bytes 9220
  554.0 333.8 %copy-start.46 = (f32[3072]{0:T(1024)S(1)}, f32[3072]{0:T(1024)}, u32[]{:S(2)}) copy-start(f32[3072]{0:T(1024)} %get-tuple-element.222) | copy-start | bytes 36868
  554.0 333.8 %copy-start.54 = (f32[768]{0:T(1024)S(1)}, f32[768]{0:T(1024)}, u32[]{:S(2)}) copy-start(f32[768]{0:T(1024)} %get-tuple-element.173) | copy-start | bytes 9220
  554.0 333.8 %copy-start.55 = (f32[768]{0:T(1024)S(1)}, f32[768]{0:T(1024)}, u32[]{:S(2)}) copy-start(f32[768]{0:T(1024)} %get-tuple-element.177) | copy-start | bytes 9220
  934.7 6.0 copy-start.5
  934.7 6.0 copy-start.35
  934.7 6.1 copy-start.39
  940.8 9.7 %copy-start.1 = (bf16[768,768]{1,0:T(8,128)(2,1)S(1)}, bf16[768,768]{1,0:T(8,128)(2,1)}, u32[]{:S(2)}) copy-start(bf16[768,768]{1,0:T(8,128)(2,1)} %param.27) | copy-start | bytes 3538948
  942.8 4.4 copy-start.33
  942.8 5.2 copy-start.32
  942.8 6.0 copy-start.31
  942.8 6.9 copy-start.30
  (34 other events, 60.4 us)
Sparse Core Ops, SparseCore 0:
  10.7 31.0 all-gather.4
  43.9 28.5 all-gather.2
  187.6 37.5 reduce-scatter.14
  227.7 37.9 reduce-scatter.16
  269.1 67.9 reduce-scatter.18
  340.4 68.1 reduce-scatter.24
  412.2 68.2 reduce-scatter.26
  483.9 68.2 reduce-scatter.28
  555.8 163.5 reduce-scatter.22
  722.8 162.5 reduce-scatter.20
  889.3 48.7 all-reduce.13
where the time goes:
time: 963 us; the launch traced here: 957 us
  waiting for transfers between devices  669 us (69%)
  matrix products  135 us (14%)
  other arithmetic  53.9 us (6%)
  blocking collectives  41.5 us (4%)
  local copies, waits for them, and re-layouts  40.1 us (4%)
  between operations  16.4 us (2%)
    unnamed x14, waiting for transfers between devices  211 us
    reduce_scatter x1, waiting for transfers between devices, local(): lax.psum_scatter(grad_outer_weight, 'seq', scatter_dimension=0, tiled=True)  165 us
    reduce_scatter x1, waiting for transfers between devices, local(): lax.psum_scatter(grad_inner_weight, 'seq', scatter_dimension=0, tiled=True)  164 us
    reduce_scatter x1, waiting for transfers between devices, local(): lax.psum_scatter(grad_output_weight, 'seq', scatter_dimension=0, tiled=True)  44.1 us
    reduce_scatter x1, waiting for transfers between devices, local(): lax.psum_scatter(grad_value_part.reshape(seq_dev, seq_tokens, width).asty...  36.3 us
    dot_general x6, matrix products, row_dot(): return jnp.dot(left, right, preferred_element_type=jnp.float32)  32.4 us
    reduce_scatter x1, waiting for transfers between devices, local(): lax.psum_scatter(grad_key_part.reshape(seq_dev, seq_tokens, width).astype...  29 us
    unnamed x1, blocking collectives  28.6 us
  transfers between devices with their start and end apart: 11, of which 10 were waited for; matrix products, arithmetic and copies ran while one was open for 10% of the time, Pallas kernels for 0%

commit v1 on v0

v1 whole, which is shorter than its diff:
```python
import itertools
import math

import jax
import jax.numpy as jnp
from jax import lax
from jax.experimental import pallas as pl
from jax.experimental.pallas import tpu as pltpu
from jax.sharding import PartitionSpec as P

HEADS = 12
HD = 64
MESH = pl.DeviceIdType.MESH
BF = jnp.bfloat16
F32 = jnp.float32
LOG2E = math.log2(math.e)
SCALE2 = 0.125 * LOG2E
EPS = 1e-05

FLOWS = 12
BITS = ("z1", "z0", "y")
ORDER_Y = ("y", "x", "z0", "z1")
ORDER_Z = ("z0", "y", "x", "z1")
ORDERS = [ORDER_Y, ORDER_Z] * 6

NAMES = ("qb", "vb", "ob", "ag", "as", "xb", "fg", "fs", "ib")


def nn(left, right):
    return jnp.dot(left, right, preferred_element_type=F32)


def nt(left, right):
    return lax.dot_general(left, right, (((1,), (1,)), ((), ())), preferred_element_type=F32)


def tn(left, right):
    return lax.dot_general(left, right, (((0,), (0,)), ((), ())), preferred_element_type=F32)


def fold8(values):
    rows, width = values.shape
    return jnp.sum(values.reshape(rows // 8, 8, width), axis=0)


def recv_shape(order, k, rows, cols):
    done = order[: k + 1]
    free = [2 for ax in BITS if ax not in done]
    return (*free, rows // 2 if "x" in done else rows, cols)


def layer_kernel(groups, names, *refs):
    r = dict(zip(names, refs))
    seq = lax.axis_index("seq")
    blk = lax.axis_index("blk")
    x = lax.div(blk, 2)
    c = lax.rem(blk, 2)
    hi = lax.div(seq, groups)
    own = {"x": x, "y": lax.rem(hi, 2), "z0": lax.rem(lax.div(hi, 2), 2), "z1": lax.div(hi, 4)}
    blk_x = blk + 2 - 4 * x
    blk_c = blk + 1 - 2 * c
    blk_xc = blk_x + 1 - 2 * c
    peers = {
        "c": (seq, blk_c),
        "x": (seq, blk_x),
        "y": (seq + (1 - 2 * own["y"]) * groups, blk),
        "z0": (seq + (1 - 2 * own["z0"]) * 2 * groups, blk),
        "z1": (seq + (1 - 2 * own["z1"]) * 4 * groups, blk),
    }
    slots, tok, width = r["xall"].shape
    seq_len = slots * tok
    half = width // 2
    ff = r["wi"].shape[1]
    pairs = half // (2 * HD)
    mine = (blk, blk_x)
    col0 = pl.multiple_of(c * half, 128)
    place = {name: width * i for i, name in enumerate(NAMES)}

    def vec(name, start=0, size=width):
        return r["vec"][:, pl.ds(place[name] + start, size)]

    def remote(src, dst, sems, i, peer):
        return pltpu.make_async_remote_copy(
            src_ref=src,
            dst_ref=dst,
            send_sem=r[sems + "_s"].at[i] if not isinstance(i, tuple) else r[sems + "_s"].at[i[0], i[1]],
            recv_sem=r[sems + "_r"].at[i] if not isinstance(i, tuple) else r[sems + "_r"].at[i[0], i[1]],
            device_id=peers[peer],
            device_id_type=MESH,
        )

    cols = pl.ds(col0, half)
    local = [
        pltpu.make_async_copy(r["hid"].at[x], r["xall"].at[blk], r["lsem"].at[0]),
        pltpu.make_async_copy(r["wq"].at[:, cols], r["wqkv"].at[0], r["lsem"].at[1]),
        pltpu.make_async_copy(r["wk"].at[:, cols], r["wqkv"].at[1], r["lsem"].at[2]),
        pltpu.make_async_copy(r["wv"].at[:, cols], r["wqkv"].at[2], r["lsem"].at[3]),
        pltpu.make_async_copy(r["go"].at[x], r["gown"].at[0], r["lsem"].at[4]),
        pltpu.make_async_copy(r["wo_in"], r["wo"], r["lsem"].at[5]),
        pltpu.make_async_copy(r["wi_in"], r["wi"], r["lsem"].at[6]),
        pltpu.make_async_copy(r["wx_in"], r["wx"], r["lsem"].at[7]),
    ]
    for copy in local:
        copy.start()

    barrier = pltpu.get_barrier_semaphore()
    for peer in peers.values():
        pl.semaphore_signal(barrier, inc=1, device_id=peer, device_id_type=MESH)
    pl.semaphore_wait(barrier, len(peers))

    def ex(i):
        if i == 0:
            return remote(r["hid"].at[1 - x], r["xall"].at[blk], "ex", 0, "x")
        if i == 1:
            return remote(r["hid"].at[x], r["xall"].at[blk], "ex", 1, "c")
        if i == 2:
            return remote(r["xall"].at[blk_x], r["xall"].at[blk_x], "ex", 2, "c")
        if i == 3:
            return remote(r["go"].at[1 - x], r["gown"].at[1], "ex", 3, "x")
        if i < 4 + pairs:
            lanes = pl.ds(pl.multiple_of(c * half + (i - 4) * 128, 128), 128)
            return remote(r["att"].at[:, :, lanes], r["att"].at[:, :, lanes], "ex", i, "c")
        i -= 4 + pairs
        if i < 2:
            return remote(r["ga"].at[mine[i]], r["ga"].at[mine[i]], "ex", i + 4 + pairs, "c")
        if i == 2:
            return remote(r["hbuf"].at[1], r["hout"].at[x], "ex", i + 4 + pairs, "x")
        if i == 3:
            return remote(r["gffn"], r["grecv"], "ex", i + 4 + pairs, "c")
        return remote(r["inn"].at[pl.ds(tok, tok)], r["gin"].at[x], "ex", i + 4 + pairs, "x")

    ex_ga, ex_hout, ex_part, ex_gin = 4 + pairs, 6 + pairs, 7 + pairs, 8 + pairs
    ex(0).start()
    ex(1).start()
    kept = jnp.where(r["dg"][x] == 2, 0.0, 1.0).astype(F32)
    r["sg8"][...] = jnp.zeros_like(r["sg8"])

    def project(j):
        rows = pl.ds(pl.multiple_of(j * tok, tok), tok)
        block = r["xall"][j]
        r["q"][rows, :] = (nn(block, r["wqkv"][0]) + r["vec"][:, pl.ds(col0, half)]).astype(BF)
        r["k"][rows, :] = nn(block, r["wqkv"][1]).astype(BF)
        r["v"][rows, :] = (
            nn(block, r["wqkv"][2]) + r["vec"][:, pl.ds(pl.multiple_of(place["vb"] + col0, 128), half)]
        ).astype(BF)

    for i in range(4):
        local[i].wait()
    project(blk)
    ex(1).wait_recv()
    project(blk_c)
    ex(0).wait_recv()
    ex(2).start()
    ex(3).start()
    project(blk_x)
    ex(2).wait_recv()
    project(blk_xc)

    for p in range(pairs):
        lanes = pl.ds(p * 128, 128)
        r["kt"][lanes, :] = r["k"][:, lanes].T
        vt = r["v"][:, lanes].T
        for h in range(2):
            r["vx"][2 * p + h, pl.ds(0, HD), :] = vt[h * HD : (h + 1) * HD]
            r["vx"][2 * p + h, pl.ds(HD, 16), :] = jnp.ones((16, seq_len), BF)

    qb = tok
    blocks = seq_len // qb
    lane_head = lax.broadcasted_iota(jnp.int32, (qb, 128), 1) // HD

    def forward(p, t):
        lanes = pl.ds(p * 128, 128)
        rows = pl.ds(pl.multiple_of(t * qb, qb), qb)
        qp = r["q"][rows, lanes]
        outs = []
        for h in range(2):
            qm = jnp.where(lane_head == h, qp, jnp.zeros_like(qp))
            st = nt(r["k"][:, lanes], qm)
            top = jnp.max(st, axis=0, keepdims=True)
            pt = jnp.exp2((st - top) * SCALE2).astype(BF)
            ot = nn(r["vx"][2 * p + h], pt)
            total = ot[HD : HD + 1]
            outs.append(ot[:HD] / total)
            r["lse"][2 * p + h, :, rows] = top * SCALE2 + jnp.log2(total)
        both = jnp.concatenate(outs, axis=0).astype(BF)
        r["att"][t, :, pl.ds(pl.multiple_of(c * half + p * 128, 128), 128)] = both.T

    for p in range(pairs):

        @pl.loop(0, blocks)
        def _(t):
            forward(p, t)

        ex(4 + p).start()

    for i in range(4, 8):
        local[i].wait()
    for p in range(pairs):
        ex(4 + p).wait_recv()
    ex(3).wait_recv()

    chunk = 32
    per = tok // chunk

    def own_rows(i):
        second = lax.div(i, per)
        slot = blk + second * (blk_x - blk)
        inner = pl.ds(pl.multiple_of(lax.rem(i, per) * chunk, chunk), chunk)
        rows = pl.ds(pl.multiple_of(i * chunk, chunk), chunk)
        return slot, second, inner, rows

    def fold_in(name, values):
        at = pl.ds(place[name], values.shape[1])
        r["sg8"][:, at] += fold8(values)

    for i in range(2):
        r["acc"][pl.ds(i * tok, tok), :] = nn(r["att"][mine[i]], r["wo"][...])

    @pl.loop(0, 2 * per)
    def _(i):
        slot, second, inner, rows = own_rows(i)
        v = r["acc"][rows, :] + vec("ob") + r["xall"][slot, inner, :].astype(F32)
        cen = v - jnp.mean(v, axis=-1, keepdims=True)
        rstd = lax.rsqrt(jnp.mean(cen * cen, axis=-1, keepdims=True) + EPS)
        xh = cen * rstd
        normed = xh * vec("ag") + vec("as")
        r["xh"][rows, :] = xh
        r["rs"][rows, :] = rstd
        r["acc"][rows, :] = normed
        r["inn"][rows, :] = normed.astype(BF)

    tile = 256

    @pl.loop(0, ff // tile)
    def _(j):
        at = pl.ds(pl.multiple_of(j * tile, tile), tile)
        bias = r["vec"][:, pl.ds(pl.multiple_of(place["ib"] + j * tile, 128), tile)]
        pre = nn(r["inn"][...], r["wi"][:, at]) + bias
        phi = 0.5 + 0.5 * lax.erf(pre * math.sqrt(0.5))
        dens = jnp.exp2(pre * pre * (-0.5 * LOG2E)) * (1.0 / math.sqrt(2.0 * math.pi))
        low = (pre * phi).astype(BF)
        r["act"][:, at] = low
        r["gp"][:, at] = (phi + pre * dens).astype(BF)
        r["acc"][...] += nn(low, r["wx"][at, :])

    @pl.loop(0, 2 * per)
    def _(i):
        slot, second, inner, rows = own_rows(i)
        xf = r["xall"][slot, inner, :].astype(F32)
        v = r["acc"][rows, :] + vec("xb")
        cen = v - jnp.mean(v, axis=-1, keepdims=True)
        rstd = lax.rsqrt(jnp.mean(cen * cen, axis=-1, keepdims=True) + EPS)
        xh = cen * rstd
        out = kept * (xh * vec("fg") + vec("fs")) + (1.0 - kept) * xf
        r["hbuf"][second, inner, :] = out.astype(BF)
        g = kept * r["gown"][second, inner, :].astype(F32)
        fold_in("fg", g * xh)
        fold_in("fs", g)
        gx = g * vec("fg")
        m1 = jnp.mean(gx, axis=-1, keepdims=True)
        m2 = jnp.mean(gx * xh, axis=-1, keepdims=True)
        gs = rstd * (gx - m1 - xh * m2)
        low = gs.astype(BF)
        r["acc"][rows, :] = gs
        r["gffn"][rows, :] = low
        fold_in("xb", low.astype(F32))

    ex(ex_hout).start()
    hout_local = pltpu.make_async_copy(r["hbuf"].at[0], r["hout"].at[x], r["lsem"].at[0])
    hout_local.start()

    def pay(f):
        return r["d2"].at[c, f] if f < 8 else r["dc"].at[f - 8]

    rows_f, cols_f = r["dc"].shape[-2:]

    def view(ref, order, k, send):
        idx = [slice(None)] * 3
        row = pl.ds(0, rows_f)
        for j, ax in enumerate(order[: k + 1]):
            want = 1 - own[ax] if (j == k and send) else own[ax]
            if ax == "x":
                row = pl.ds(pl.multiple_of(want * (rows_f // 2), 16), rows_f // 2)
            else:
                idx[BITS.index(ax)] = want
        return (*idx, row, slice(None))

    def hop(f, k):
        order = ORDERS[f]
        at = view(None, order, k, True)
        return remote(pay(f).at[at], r[f"r{f}_{k}"], "rs", (f, k), order[k])

    def add_in(f, k):
        order = ORDERS[f]
        idx = list(view(None, order, k, False))
        ref = pay(f)
        free = [ax for ax in BITS if ax not in order[: k + 1]]
        for combo in itertools.product((0, 1), repeat=len(free)):
            for ax, bit in zip(free, combo):
                idx[BITS.index(ax)] = bit
            at = tuple(idx)
            got = r[f"r{f}_{k}"][(*combo, slice(None), slice(None))]
            ref[at] = ref[at] + got

    x_rows = pl.ds(pl.multiple_of(x * (rows_f // 2), 16), rows_f // 2)

    def spread(f, k):
        if k == 0:
            part = r["fin"].at[f, c, x_rows]
            return remote(part, part, "rs", (f, 4), "x")
        part = r["fin"].at[f, c]
        return remote(part, part, "rs", (f, 5), "c")

    def d2d(f):
        return remote(r["d2"].at[1 - c, f], r["rc"].at[f], "rs", (f, 6), "c")

    def step(f, k):
        order = ORDERS[f]
        if k == -1:
            d2d(f).wait_recv()
            for combo in itertools.product((0, 1), repeat=3):
                ref = pay(f)
                ref[combo] = ref[combo] + r["rc"][(f, *combo)]
            hop(f, 0).start()
        elif k == 0:
            hop(f, 0).start()
        elif k < 4:
            hop(f, k - 1).wait_recv()
            add_in(f, k - 1)
            hop(f, k).start()
        elif k == 4:
            hop(f, 3).wait_recv()
            add_in(f, 3)
            r["fin"][f, c, x_rows, :] = pay(f)[(own["z1"], own["z0"], own["y"], x_rows, slice(None))]
            spread(f, 0).start()
        elif k == 5:
            spread(f, 0).wait_recv()
            spread(f, 1).start()
        else:
            spread(f, 1).wait_recv()

    bits8 = [(a, b, d) for a in range(2) for b in range(2) for d in range(2)]
    outer_rows = ff // 8

    @pl.loop(0, 8)
    def _(j):
        at = r["act"][:, pl.ds(pl.multiple_of(j * outer_rows, 128), outer_rows)]
        val = tn(at, r["gffn"][...]).astype(BF)
        i1, i2, i3 = lax.div(j, 4), lax.rem(lax.div(j, 2), 2), lax.rem(j, 2)
        for f in range(4):
            for h in range(2):
                r["d2"][h, f, i1, i2, i3] = val[f * rows_f : (f + 1) * rows_f, h * cols_f : (h + 1) * cols_f]

    for f in range(4):
        d2d(f).start()

    r["innt"][...] = r["inn"][...].T
    per_half = (ff // 2) // 128

    def inner_tile(j):
        at = pl.ds(pl.multiple_of(j * tile, tile), tile)
        dact = nt(r["gffn"][...], r["wx"][at, :])
        gpre = (dact * r["gp"][:, at].astype(F32)).astype(BF)
        r["sg8"][:, pl.ds(pl.multiple_of(place["ib"] + j * tile, 128), tile)] = fold8(gpre.astype(F32))
        val = nn(r["innt"][...], gpre).astype(BF)
        for g2 in range(tile // 128):
            g = (tile // 128) * j + g2
            rest = lax.rem(g, per_half)
            f = 4 + lax.div(rest, cols_f // 128)
            lane = pl.multiple_of(lax.rem(rest, cols_f // 128) * 128, 128)
            piece = val[:, g2 * 128 : (g2 + 1) * 128]
            r["d2"][lax.div(g, per_half), f, :, :, :, :, pl.ds(lane, 128)] = piece.reshape(2, 2, 2, rows_f, 128)
        r["acc"][...] += nt(gpre, r["wi"][:, at])

    tiles = ff // tile
    for part in range(2):

        @pl.loop(part * tiles // 2, (part + 1) * tiles // 2)
        def _(j):
            inner_tile(j)

        for f in ((0, 1), (2, 3))[part]:
            step(f, -1)

    for f in range(4, 8):
        d2d(f).start()

    @pl.loop(0, 2 * per)
    def _(i):
        slot, second, inner, rows = own_rows(i)
        g = r["acc"][rows, :]
        xh = r["xh"][rows, :]
        fold_in("ag", g * xh)
        fold_in("as", g)
        gx = g * vec("ag")
        m1 = jnp.mean(gx, axis=-1, keepdims=True)
        m2 = jnp.mean(gx * xh, axis=-1, keepdims=True)
        gs = r["rs"][rows, :] * (gx - m1 - xh * m2)
        low = gs.astype(BF)
        r["acc"][rows, :] = gs
        r["ga"][slot, inner, :] = low
        fold_in("ob", low.astype(F32))

    ex(ex_ga).start()
    ex(ex_ga + 1).start()
    for f in range(4, 8):
        step(f, -1)

    do = r["wx"].at[pl.ds(0, seq_len), pl.ds(0, half)]
    dq = r["wx"].at[pl.ds(0, seq_len), pl.ds(half, half)]
    dk = r["wx"].at[pl.ds(seq_len, seq_len), pl.ds(0, half)]
    dv = r["wx"].at[pl.ds(seq_len, seq_len), pl.ds(half, half)]
    wo_own = r["wo"].at[pl.ds(pl.multiple_of(c * half, 128), half), :]

    def upstream(slot):
        rows = pl.ds(pl.multiple_of(slot * tok, tok), tok)
        do[rows, :] = nt(r["ga"][slot], wo_own[...]).astype(BF)

    upstream(blk)
    upstream(blk_x)
    ex(ex_ga).wait_recv()
    ex(ex_ga + 1).wait_recv()
    upstream(blk_c)
    upstream(blk_xc)

    for p in range(pairs):
        lanes = pl.ds(p * 128, 128)
        at = r["att"][:, :, pl.ds(pl.multiple_of(c * half + p * 128, 128), 128)].reshape(seq_len, 128)
        prod = (at.astype(F32) * do[:, lanes].astype(F32)).T
        for h in range(2):
            r["delta"][2 * p + h] = jnp.sum(prod[h * HD : (h + 1) * HD], axis=0, keepdims=True)

    att_all = r["att"][...].reshape(seq_len, width)
    ga_cols = r["ga"][:, :, pl.ds(col0, half)].reshape(seq_len, half)
    r["dc"][3] = tn(att_all, ga_cols).astype(BF).reshape(2, 2, 2, rows_f, cols_f)

    def backward(p, t):
        lanes = pl.ds(p * 128, 128)
        rows = pl.ds(pl.multiple_of(t * qb, qb), qb)
        qp = r["q"][rows, lanes]
        dp = do[rows, lanes]
        kp = r["k"][:, lanes]
        vp = r["v"][:, lanes]
        zero = jnp.zeros_like(qp)
        dqs = []
        for h in range(2):
            qm = jnp.where(lane_head == h, qp, zero)
            dm = jnp.where(lane_head == h, dp, zero)
            pt = jnp.exp2(nt(kp, qm) * SCALE2 - r["lse"][2 * p + h, :, rows])
            dpt = nt(vp, dm)
            ds = (pt * (dpt - r["delta"][2 * p + h, :, rows])).astype(BF)
            r["dva"][...] += nn(pt.astype(BF), dm)
            r["dka"][...] += nn(ds, qm)
            dqs.append(nn(r["kt"][pl.ds(p * 128 + h * HD, HD), :], ds))
        both = (jnp.concatenate(dqs, axis=0) * 0.125).astype(BF)
        dq[rows, lanes] = both.T

    later = {
        0: [(f, 1) for f in range(0, 4)],
        1: [(f, 1) for f in range(4, 8)] + [(f, 2) for f in range(0, 4)],
        2: [(f, 2) for f in range(4, 8)] + [(f, 3) for f in range(0, 4)],
    }
    for p in range(pairs):
        r["dka"][...] = jnp.zeros_like(r["dka"])
        r["dva"][...] = jnp.zeros_like(r["dva"])

        @pl.loop(0, blocks)
        def _(t):
            backward(p, t)

        lanes = pl.ds(p * 128, 128)
        dk[:, lanes] = (r["dka"][...] * 0.125).astype(BF)
        dv[:, lanes] = r["dva"][...].astype(BF)
        for f, k in later[p]:
            step(f, k)

    xt = r["wi"].at[:, pl.ds(0, seq_len)]
    xt[...] = r["xall"][...].reshape(seq_len, width).T
    for i, g in enumerate((dq, dk, dv)):
        r["dc"][i] = nn(xt[...], g[...]).astype(BF).reshape(2, 2, 2, rows_f, cols_f)
        step(8 + i, 0)
    step(11, 0)
    r["sg8"][:, pl.ds(col0, half)] = fold8(dq[...].astype(F32))
    r["sg8"][:, pl.ds(pl.multiple_of(place["vb"] + col0, 128), half)] = fold8(dv[...].astype(F32))
    r["sgs"][0] = jnp.sum(r["sg8"][...], axis=0, keepdims=True)

    def small(k):
        return remote(r["sgs"].at[k], r["sgr"].at[k], "sm", k, ("c", "x", "y", "z0", "z1")[k])

    small(0).start()

    def partial(slot):
        rows = pl.ds(pl.multiple_of(slot * tok, tok), tok)
        return (
            nt(dq[rows, :], r["wqkv"][0]) + nt(dk[rows, :], r["wqkv"][1]) + nt(dv[rows, :], r["wqkv"][2])
        )

    r["gffn"][pl.ds(0, tok), :] = partial(blk_c).astype(BF)
    r["gffn"][pl.ds(tok, tok), :] = partial(blk_xc).astype(BF)
    ex(ex_part).start()
    for i in range(2):
        rows = pl.ds(i * tok, tok)
        r["acc"][rows, :] += partial(mine[i])
    ex(ex_part).wait_recv()
    for i in range(2):
        rows = pl.ds(i * tok, tok)
        total = r["acc"][rows, :] + r["grecv"][rows, :].astype(F32) + (1.0 - kept) * r["gown"][i].astype(F32)
        r["inn"][rows, :] = total.astype(BF)
    ex(ex_gin).start()
    gin_local = pltpu.make_async_copy(r["inn"].at[pl.ds(0, tok)], r["gin"].at[x], r["lsem"].at[1])
    gin_local.start()

    for k in range(5):
        small(k).wait_recv()
        r["sgs"][k + 1] = r["sgs"][k] + r["sgr"][k]
        if k < 4:
            small(k + 1).start()
    r["sout"][...] = r["sgs"][5]

    rest = [[(f, 3) for f in range(4, 8)], [(f, 4) for f in range(0, 8)], [(f, 5) for f in range(0, 8)]]
    rest += [[(f, k) for f in range(8, 12)] for k in range(1, 6)]
    rest += [[(f, 6) for f in range(12)]]
    for group in rest:
        for f, k in group:
            step(f, k)

    ex(ex_hout).wait_recv()
    ex(ex_gin).wait_recv()
    hout_local.wait()
    gin_local.wait()
    for i in range(9 + pairs):
        ex(i).wait_send()
    for k in range(5):
        small(k).wait_send()
    for f in range(FLOWS):
        for k in range(4):
            hop(f, k).wait_send()
        spread(f, 0).wait_send()
        spread(f, 1).wait_send()
        if f < 8:
            d2d(f).wait_send()


def build(mesh):
    n_seq = mesh.shape["seq"]
    groups = n_seq // 8

    def local(
        hidden_in,
        depth_group,
        query_weight,
        query_bias,
        key_weight,
        value_weight,
        value_bias,
        output_weight,
        output_bias,
        attn_gain,
        attn_shift,
        inner_weight,
        inner_bias,
        outer_weight,
        outer_bias,
        final_gain,
        final_shift,
        grad_out,
    ):
        seqs, tok, width = hidden_in.shape
        ff = inner_weight.shape[1]
        slots = mesh.shape["blk"]
        seq_len = slots * tok
        half = width // 2
        heads = half // HD
        rows_f, cols_f = width // 8, half
        vec = jnp.concatenate(
            [query_bias, value_bias, output_bias, attn_gain, attn_shift, outer_bias, final_gain, final_shift, inner_bias]
        ).astype(F32)[None]
        small = vec.shape[1]
        hbm = pl.BlockSpec(memory_space=pl.ANY)
        vmem = pl.BlockSpec(memory_space=pltpu.VMEM)
        ins = [
            ("dg", depth_group, pl.BlockSpec(memory_space=pltpu.SMEM)),
            ("vec", vec, vmem),
            ("hid", hidden_in, hbm),
            ("go", grad_out, hbm),
            ("wq", query_weight, hbm),
            ("wk", key_weight, hbm),
            ("wv", value_weight, hbm),
            ("wo_in", output_weight, hbm),
            ("wi_in", inner_weight, hbm),
            ("wx_in", outer_weight, hbm),
        ]
        outs = [
            ("hout", (seqs, tok, width), BF, hbm),
            ("gin", (seqs, tok, width), BF, hbm),
            ("fin", (FLOWS, 2, rows_f, cols_f), BF, vmem),
            ("sout", (1, small), F32, vmem),
        ]
        v = pltpu.VMEM
        dma = pltpu.SemaphoreType.DMA
        pairs = half // 128
        scratch = [
            ("xall", v((slots, tok, width), BF)),
            ("gown", v((2, tok, width), BF)),
            ("wqkv", v((3, width, half), BF)),
            ("wo", v((width, width), BF)),
            ("wi", v((width, ff), BF)),
            ("wx", v((ff, width), BF)),
            ("q", v((seq_len, half), BF)),
            ("k", v((seq_len, half), BF)),
            ("v", v((seq_len, half), BF)),
            ("kt", v((half, seq_len), BF)),
            ("vx", v((heads, HD + 16, seq_len), BF)),
            ("lse", v((heads, 1, seq_len), F32)),
            ("delta", v((heads, 1, seq_len), F32)),
            ("att", v((slots, tok, width), BF)),
            ("ga", v((slots, tok, width), BF)),
            ("act", v((2 * tok, ff), BF)),
            ("gp", v((2 * tok, ff), BF)),
            ("inn", v((2 * tok, width), BF)),
            ("innt", v((width, 2 * tok), BF)),
            ("gffn", v((2 * tok, width), BF)),
            ("xh", v((2 * tok, width), F32)),
            ("acc", v((2 * tok, width), F32)),
            ("rs", v((2 * tok, 1), F32)),
            ("hbuf", v((2, tok, width), BF)),
            ("grecv", v((2 * tok, width), BF)),
            ("dka", v((seq_len, 128), F32)),
            ("dva", v((seq_len, 128), F32)),
            ("d2", v((2, 8, 2, 2, 2, rows_f, cols_f), BF)),
            ("rc", v((8, 2, 2, 2, rows_f, cols_f), BF)),
            ("dc", v((4, 2, 2, 2, rows_f, cols_f), BF)),
            ("sg8", v((8, small), F32)),
            ("sgs", v((6, 1, small), F32)),
            ("sgr", v((5, 1, small), F32)),
            ("lsem", dma((8,))),
            ("ex_s", dma((9 + pairs,))),
            ("ex_r", dma((9 + pairs,))),
            ("rs_s", dma((FLOWS, 7))),
            ("rs_r", dma((FLOWS, 7))),
            ("sm_s", dma((5,))),
            ("sm_r", dma((5,))),
        ]
        for f in range(FLOWS):
            for k in range(4):
                scratch.append((f"r{f}_{k}", v(recv_shape(ORDERS[f], k, rows_f, cols_f), BF)))
        names = [e[0] for e in ins] + [e[0] for e in outs] + [e[0] for e in scratch]

        def body(*refs):
            layer_kernel(groups, names, *refs)

        hout, gin, fin, sout = pl.pallas_call(
            body,
            out_shape=[jax.ShapeDtypeStruct(e[1], e[2]) for e in outs],
            in_specs=[e[2] for e in ins],
            out_specs=[e[3] for e in outs],
            scratch_shapes=[e[1] for e in scratch],
            compiler_params=pltpu.CompilerParams(
                collective_id=0, has_side_effects=True, vmem_limit_bytes=64 * 1024 * 1024
            ),
            name="layer",
        )(*[e[1] for e in ins])

        def across(values):
            if groups == 1:
                return values
            rows = [[g * groups + i for i in range(groups)] for g in range(8)]
            return lax.psum_scatter(values, "seq", scatter_dimension=0, axis_index_groups=rows, tiled=True)

        def sides(part):
            return jnp.concatenate([part[0], part[1]], axis=-1)

        wide = fin.astype(F32)
        g_outer = across(jnp.concatenate([sides(wide[f]) for f in range(4)], axis=0))
        g_inner = across(jnp.concatenate([wide[f, h] for h in range(2) for f in range(4, 8)], axis=-1))
        g_q, g_k, g_v, g_o = [across(sides(wide[f])) for f in range(8, 12)]
        if groups > 1:
            rows = [[g * groups + i for i in range(groups)] for g in range(8)]
            sout = lax.psum(sout, "seq", axis_index_groups=rows)
        seq = lax.axis_index("seq")
        flat = sout[0]

        def share(i, size):
            return lax.dynamic_slice(flat, (i * width + seq * (size // n_seq),), (size // n_seq,))

        s = [share(i, width) for i in range(8)] + [share(8, ff)]
        return (
            hout,
            gin,
            g_q,
            s[0],
            g_k,
            g_v,
            s[1],
            g_o,
            s[2],
            s[3],
            s[4],
            g_inner,
            s[8],
            g_outer,
            s[5],
            s[6],
            s[7],
        )

    return local


def solution(mesh):
    rows = P("seq", "blk", None)
    placed = (rows, P("seq"), *([P()] * 15), rows)
    mat, one = P("seq", None), P("seq")
    return jax.shard_map(
        build(mesh),
        mesh=mesh,
        in_specs=placed,
        out_specs=(rows, rows, mat, one, mat, mat, one, mat, one, one, one, mat, one, mat, one, one, one),
        check_vma=False,
    )
```

time: 963 us -> 193 us (0.20)
  waiting for transfers between devices: 669 us -> 0 us
  Pallas kernels: 0 us -> 175 us
  matrix products: 135 us -> 0 us
  other arithmetic: 53.9 us -> 5.31 us
  blocking collectives: 41.5 us -> 0 us
  local copies, waits for them, and re-layouts: 40.1 us -> 11.7 us
  between operations: 16.4 us -> 0.77 us
    reduce_scatter x5 -> x0, waiting for transfers between devices: 439 us -> none  [the longest x1 165 us: local(): lax.psum_scatter(grad_outer_weight, 'seq', scatter_dimension=0, tiled=True)]
    unnamed x14 -> x0, waiting for transfers between devices: 211 us -> none
    pallas_call x0 -> x1, Pallas kernels: none -> 175 us  [local(): pl.pallas_call(body, out_shape=[jax.ShapeDtypeStruct(e[1], e[2]) for e in...]
    dot_general x30 -> x0, matrix products: 135 us -> none  [the longest x6 32.4 us: row_dot(): return jnp.dot(left, right, preferred_element_type=jnp.float32)]
    convert_element_type x27 -> x2, other arithmetic: 35.5 us -> 2.52 us  [the longest x1 1.87 us: local(): wide = fin.astype(F32)]
    unnamed x1 -> x0, blocking collectives: 28.6 us -> none
    all_gather x2 -> x0, waiting for transfers between devices: 19.7 us -> none  [the longest x1 18.3 us: local(): lax.all_gather(keys_local, 'blk', axis=1, tiled=True)]
    reduce_sum x11 -> x0, other arithmetic: 17.7 us -> none  [the longest x1 11 us: local(): new_sum = jnp.sum(weights, axis=-1)]
  transfers between devices with their start and end apart: 11 -> 0, of which waited for: 10 -> 0; matrix products, arithmetic and copies ran while one was open for 10% -> 0% of each run, Pallas kernels for 0% -> 0%
where the time goes in v1:
time: 193 us
  Pallas kernels  175 us (91%)
  local copies, waits for them, and re-layouts  11.7 us (6%)
  other arithmetic  5.31 us (3%)
    pallas_call x1, Pallas kernels, local(): pl.pallas_call(body, out_shape=[jax.ShapeDtypeStruct(e[1], e[2]) for e in...  175 us
    unnamed x23, local copies, waits for them, and re-layouts  8.21 us

profile of v1, /device:TPU:1, one launch (start us, length us, event | category | flops | bytes accessed | tf_op | source)
XLA Modules:
  0.0 192.9 jit_solution(11559070170185199906)
XLA Ops:
  0.7 0.7 constant_dynamic-update-slice_fusion.8
  1.3 0.7 constant_dynamic-update-slice_fusion.7
  2.0 0.7 constant_dynamic-update-slice_fusion.6
  2.7 0.7 constant_dynamic-update-slice_fusion.5
  3.4 0.7 constant_dynamic-update-slice_fusion.4
  4.1 0.7 constant_dynamic-update-slice_fusion.3
  4.8 0.7 constant_dynamic-update-slice_fusion.2
  5.5 0.7 constant_dynamic-update-slice_fusion.1
  6.2 0.7 constant_dynamic-update-slice_fusion
  6.9 0.7 convert_element_type.13.refs_1_
  7.5 175.1 %layer.1 = (bf16[2,256,768]{2,1,0:T(8,128)(2,1)}, bf16[2,256,768]{2,1,0:T(8,128)(2,1)}, bf16[12,2,96,384]{3,2,1,0:T(8,128)(2,1)}, f32[1,9216]{1,0:T(1,128)}) custom-call(s32[2]{0:T(128)} %refs_0_.1, f32[1,9216]{1,0:T(1,128)} %convert_element_type.13.refs_1_, bf16[2,256,768]{2,1,0:T(8,128)(2,1)} %refs_2_.1, bf16[2,256,768]{2,1,0:T(8,128)(2,1)} %refs_3_.1, ...), custom_call_target="tpu_custom_call" | custom-call | tf_op jit(solution)/shard_map/layer/pallas_call | solution.py:652
  182.6 1.4 fusion.16
  184.0 1.3 fusion.8
  185.2 1.9 convert_element_type.14
  187.3 0.0 copy-start.2
  187.3 0.2 slice_bitcast_fusion.7
  187.5 0.8 copy-done.2
  188.3 1.1 maximum_maximum_fusion
  189.4 0.0 copy-start.1
  189.4 0.8 pad_maximum_fusion.2
  190.2 0.0 copy-start
  190.3 0.8 pad_maximum_fusion
  191.1 0.0 copy-done.1
  191.1 0.9 copy.52
  192.0 0.0 copy-done
  192.0 0.9 copy.53
  (8 shorter events, 0.1 us)
Async XLA Ops:
  187.3 1.0 copy-start.2
  189.4 1.7 copy-start.1
  190.2 1.7 copy-start
